TPU v7x, 1024 devices: a whole 4x8x16 slice. The times are simulated.
1024 devices in a mesh: node: 32 (over z, core), local: 32 (over x, y).
Axes of the slice: x: 4, y: 8, z: 16, core: 2. Of those that a mesh axis runs over, the one named last changes fastest.
Arguments:
- tokens: bfloat16 [3072, 2048], P('node', 'local'), may hold values from -6 to 6
- grad_out: bfloat16 [3072, 2048], P('node', 'local'), may hold values from -1.1953125 to 1.1953125
- probs: bfloat16 [3072, 8], P('node'), may hold values from 0.019897461 to 0.5
- slot_of: int32 [3072, 8], P('node'), may hold values from 0 to 255, all different within a row; in each aligned block of 96 rows (0 to 95, 96 to 191, ...) at most 6 rows name the same one
- w_gate: bfloat16 [1024, 2048, 192], P(('node', 'local')), may hold values from -0.125 to 0.125
- w_up: bfloat16 [1024, 2048, 192], P(('node', 'local')), may hold values from -0.125 to 0.125
- w_down: bfloat16 [1024, 192, 2048], P(('node', 'local')), may hold values from -0.21875 to 0.21875
Outputs:
- d_tokens: bfloat16 [3072, 2048], P('node', 'local')
- d_probs: float32 [3072, 8], P('node')
- grad_gate: bfloat16 [1024, 2048, 192], P(('node', 'local'))
Inputs may be any that keep to these rules, and one draw needn't show every extreme that they name: `slot_of`: each token names 8 different slots. Among the 96 tokens of one index of node (aligned blocks of rows), no slot is named by more than 6 tokens, and in some block some slot is named by exactly 6.
All inputs are finite; a program needn't handle non-finite values.
Results may differ from a plain program's by a relative error of at most 0.0057.
Values may be sent and summed in bfloat16 or wider, within the bound.
A program may use at most 32 MiB of HBM per device.

v0:
```python
import jax
import jax.numpy as jnp
from jax import lax
from jax.sharding import PartitionSpec as P


def gated_parts(gate):
    sigmoid_gate = jax.nn.sigmoid(gate)
    return (gate * sigmoid_gate, sigmoid_gate * (1.0 + gate * (1.0 - sigmoid_gate)))


def slot_ranks(slot_of, slot_count):
    tok_node = slot_of.shape[0]
    slot_ids = jnp.arange(slot_count, dtype=jnp.int32)
    named = jnp.zeros((tok_node, slot_count), jnp.bfloat16)
    for column in range(slot_of.shape[1]):
        named = named + (slot_of[:, column][:, None] == slot_ids[None, :]).astype(jnp.bfloat16)
    row_ids = jnp.arange(tok_node, dtype=jnp.int32)
    earlier = (row_ids[None, :] < row_ids[:, None]).astype(jnp.bfloat16)
    before = jnp.dot(earlier, named, preferred_element_type=jnp.float32).astype(jnp.int32)
    return jnp.take_along_axis(before, slot_of, axis=1).reshape(tok_node * slot_of.shape[1])


def body(tokens, grad_out, probs, slot_of, w_gate, w_up, w_down):
    node_count = lax.axis_size("node")
    local_count = lax.axis_size("local")
    group_count = local_count // 4
    slot_count = node_count * group_count
    tok_node, width_local = tokens.shape
    top_count = slot_of.shape[1]
    width = width_local * local_count
    capacity = min(tok_node, 2 * tok_node * top_count // slot_count)
    pair_count = tok_node * top_count
    buffer_rows = node_count * capacity * group_count
    flat_slot = slot_of.reshape(pair_count)
    ranks = slot_ranks(slot_of, slot_count)
    position = (
        flat_slot // group_count * (capacity * group_count)
        + ranks * group_count
        + flat_slot % group_count
    )
    owners = (
        jnp.full((buffer_rows,), pair_count, jnp.int32)
        .at[position]
        .set(jnp.arange(pair_count, dtype=jnp.int32))
    )
    valid = owners < pair_count
    safe = jnp.minimum(owners, pair_count - 1)
    token_index = safe // top_count
    zero_rows = jnp.zeros((buffer_rows, width_local), tokens.dtype)
    send_input = jnp.where(valid[:, None], tokens[token_index], zero_rows).reshape(
        node_count, capacity * group_count, width_local
    )
    send_grad = jnp.where(valid[:, None], grad_out[token_index], zero_rows).reshape(
        node_count, capacity * group_count, width_local
    )
    send_weight = jnp.where(
        valid, probs.reshape(pair_count)[safe], jnp.zeros((buffer_rows,), probs.dtype)
    ).reshape(node_count, capacity * group_count)
    recv_input, recv_grad, recv_weight = (
        lax.all_to_all(send_input, "node", split_axis=0, concat_axis=0, tiled=True),
        lax.all_to_all(send_grad, "node", split_axis=0, concat_axis=0, tiled=True),
        lax.all_to_all(send_weight, "node", split_axis=0, concat_axis=0, tiled=True),
    )
    fan_shape = (node_count, capacity, group_count, 4, width_local)
    fan_input = jnp.broadcast_to(
        recv_input.reshape(node_count, capacity, group_count, 1, width_local), fan_shape
    ).reshape(node_count, capacity, local_count, width_local)
    fan_grad = jnp.broadcast_to(
        recv_grad.reshape(node_count, capacity, group_count, 1, width_local), fan_shape
    ).reshape(node_count, capacity, local_count, width_local)
    input_rows, grad_rows = (
        lax.all_to_all(fan_input, "local", split_axis=2, concat_axis=2, tiled=True),
        lax.all_to_all(fan_grad, "local", split_axis=2, concat_axis=2, tiled=True),
    )
    row_count = node_count * capacity
    input_rows = input_rows.reshape(row_count, width)
    grad_rows = grad_rows.reshape(row_count, width)
    local_index = lax.axis_index("local")
    my_group = local_index // 4
    weight_rows = lax.dynamic_index_in_dim(
        recv_weight.reshape(node_count, capacity, group_count), my_group, 2, keepdims=False
    ).reshape(row_count)
    gate_matrix = w_gate[0]
    up_matrix = w_up[0]
    down_matrix = w_down[0]
    transposed = (((1,), (1,)), ((), ()))
    gate = jnp.dot(input_rows, gate_matrix, preferred_element_type=jnp.float32)
    up_proj = jnp.dot(input_rows, up_matrix, preferred_element_type=jnp.float32)
    silu_gate, silu_slope = gated_parts(gate)
    hidden = (silu_gate * up_proj).astype(jnp.bfloat16)
    out_part = jnp.dot(hidden, down_matrix, preferred_element_type=jnp.float32)
    prob_part = jnp.sum(grad_rows.astype(jnp.float32) * out_part, axis=1)
    d_out = (weight_rows.astype(jnp.float32)[:, None] * grad_rows.astype(jnp.float32)).astype(
        jnp.bfloat16
    )
    d_hidden = lax.dot_general(d_out, down_matrix, transposed, preferred_element_type=jnp.float32)
    d_gate = (d_hidden * up_proj * silu_slope).astype(jnp.bfloat16)
    d_up = (d_hidden * silu_gate).astype(jnp.bfloat16)
    input_part = lax.dot_general(
        d_gate, gate_matrix, transposed, preferred_element_type=jnp.float32
    ) + lax.dot_general(d_up, up_matrix, transposed, preferred_element_type=jnp.float32)
    gate_grad = lax.dot_general(
        input_rows, d_gate, (((0,), (0,)), ((), ())), preferred_element_type=jnp.float32
    ).astype(jnp.bfloat16)
    send_back = input_part.reshape(node_count, capacity, local_count, width_local)
    send_prob = jnp.broadcast_to(
        prob_part.reshape(node_count, capacity, 1), (node_count, capacity, local_count)
    )
    back_input, back_prob = (
        lax.all_to_all(send_back, "local", split_axis=2, concat_axis=2, tiled=True),
        lax.all_to_all(send_prob, "local", split_axis=2, concat_axis=2, tiled=True),
    )
    summed_input = jnp.sum(
        back_input.reshape(node_count, capacity, group_count, 4, width_local), axis=3
    ).reshape(node_count, capacity * group_count, width_local)
    summed_prob = jnp.sum(back_prob.reshape(node_count, capacity, group_count, 4), axis=3).reshape(
        node_count, capacity * group_count
    )
    home_input, home_prob = (
        lax.all_to_all(summed_input, "node", split_axis=0, concat_axis=0, tiled=True),
        lax.all_to_all(summed_prob, "node", split_axis=0, concat_axis=0, tiled=True),
    )
    pair_input = home_input.reshape(buffer_rows, width_local)[position].reshape(
        tok_node, top_count, width_local
    )
    d_tokens = jnp.sum(pair_input, axis=1).astype(jnp.bfloat16)
    d_probs = home_prob.reshape(buffer_rows)[position].reshape(tok_node, top_count)
    return (d_tokens, d_probs, gate_grad[None])


def solution(mesh):
    in_specs = (
        P("node", "local"),
        P("node", "local"),
        P("node", None),
        P("node", None),
        P(("node", "local"), None, None),
        P(("node", "local"), None, None),
        P(("node", "local"), None, None),
    )
    out_specs = (P("node", "local"), P("node", None), P(("node", "local"), None, None))
    return jax.shard_map(body, mesh=mesh, in_specs=in_specs, out_specs=out_specs, check_vma=False)
```

profile of v0, /device:TPU:1, one launch (start us, length us, event | category | flops | bytes accessed | tf_op | source)
XLA Modules:
  0.0 319.3 jit_solution(3323313609824844415)
XLA Ops:
  3.6 6.3 %gather_fusion.5 = s32[768]{0:T(1024)S(1)} fusion(s32[96,256]{1,0:T(8,128)S(1)} %convolution_convert_fusion.1, s32[768]{0:T(1024)S(1)} %reshape.302), kind=kCustom, calls=%fused_computation.5 | custom fusion | bytes 12288 | tf_op jit(solution)/shard_map/jit(take_along_axis)/gather | solution.py:21
  10.4 3.4 %scatter_custom_fusion = s32[1536]{0:T(1024)S(1)} fusion(s32[768]{0:T(1024)S(1)} %fusion.51, s32[768]{0:T(1024)S(1)} %iota.14, s32[]{:T(128)} %constant.73.clone.1), kind=kCustom, calls=%fused_computation.91 | custom fusion | bytes 6148 | tf_op jit(solution)/shard_map/scatter | solution.py:45
  14.1 9.5 %gather_fusion = bf16[1536]{0:T(1024)(128)(2,1)S(1)} fusion(bf16[768]{0:T(1024)(128)(2,1)S(1)} %reshape.247, s32[2048]{0:T(1024)S(1)} %get-tuple-element.41), kind=kCustom, calls=%fused_computation | custom fusion | bytes 12288 | tf_op jit(solution)/shard_map/gather | solution.py:58
  24.3 20.4 %all-to-all-start = ((bf16[32,1,48]{2,1,0:T(2,128)(2,1)}), bf16[32,1,48]{2,1,0:T(2,128)(2,1)S(1)}, u32[]{:S(2)}, u32[]{:S(2)}) async-start(bf16[32,1,48]{2,1,0:T(2,128)(2,1)} %all_to_all.44), calls=%async_computation | async-start | bytes 32768 | tf_op jit(solution)/shard_map/all_to_all | solution.py:63
  45.0 3.2 %gather_fusion.1 = bf16[1536,64]{1,0:T(8,128)(2,1)S(1)} fusion(bf16[96,64]{1,0:T(8,128)(2,1)S(1)} %copy.137, s32[2048]{0:T(1024)S(1)} %get-tuple-element.40), kind=kCustom, calls=%fused_computation.1 | custom fusion | bytes 399360 | tf_op jit(solution)/shard_map/gather | solution.py:54
  48.2 3.2 %gather_fusion.2 = bf16[1536,64]{1,0:T(8,128)(2,1)S(1)} fusion(bf16[96,64]{1,0:T(8,128)(2,1)S(1)} %copy.140, s32[2048]{0:T(1024)S(1)} %get-tuple-element.40), kind=kCustom, calls=%fused_computation.2 | custom fusion | bytes 399360 | tf_op jit(solution)/shard_map/gather | solution.py:51
  52.7 3.8 %all-to-all-done = bf16[32,1,48]{2,1,0:T(2,128)(2,1)S(1)} async-done(((bf16[32,1,48]{2,1,0:T(2,128)(2,1)}), bf16[32,1,48]{2,1,0:T(2,128)(2,1)S(1)}, u32[]{:S(2)}, u32[]{:S(2)}) %all-to-all-start) | async-done | bytes 3104 | tf_op jit(solution)/shard_map/all_to_all | solution.py:63
  56.4 8.4 %all-to-all-start.1 = ((bf16[32,2,1536]{2,1,0:T(2,128)(2,1)}), bf16[32,2,1536]{2,1,0:T(2,128)(2,1)S(1)}, u32[]{:S(2)}, u32[]{:S(2)}) async-start(bf16[32,2,1536]{2,1,0:T(2,128)(2,1)} %reshape.336), calls=%async_computation.1 | async-start | bytes 393216 | tf_op jit(solution)/shard_map/all_to_all | solution.py:62
  65.8 17.7 %all-to-all-done.1 = bf16[32,2,1536]{2,1,0:T(2,128)(2,1)S(1)} async-done(((bf16[32,2,1536]{2,1,0:T(2,128)(2,1)}), bf16[32,2,1536]{2,1,0:T(2,128)(2,1)S(1)}, u32[]{:S(2)}, u32[]{:S(2)}) %all-to-all-start.1) | async-done | bytes 196640 | tf_op jit(solution)/shard_map/all_to_all | solution.py:62
  83.5 5.2 %all-to-all-start.3 = ((bf16[32,2,1536]{2,1,0:T(2,128)(2,1)}), bf16[32,2,1536]{2,1,0:T(2,128)(2,1)S(1)}, u32[]{:S(2)}, u32[]{:S(2)}) async-start(bf16[32,2,1536]{2,1,0:T(2,128)(2,1)} %reshape.340), calls=%async_computation.3 | async-start | bytes 393216 | tf_op jit(solution)/shard_map/all_to_all | solution.py:61
  91.3 16.2 %all-to-all-done.3 = bf16[32,2,1536]{2,1,0:T(2,128)(2,1)S(1)} async-done(((bf16[32,2,1536]{2,1,0:T(2,128)(2,1)}), bf16[32,2,1536]{2,1,0:T(2,128)(2,1)S(1)}, u32[]{:S(2)}, u32[]{:S(2)}) %all-to-all-start.3) | async-done | bytes 196640 | tf_op jit(solution)/shard_map/all_to_all | solution.py:61
  107.5 9.7 %all-to-all-start.2 = ((bf16[32,2,6144]{2,1,0:T(2,128)(2,1)}), bf16[32,2,6144]{2,1,0:T(2,128)(2,1)S(1)}, u32[]{:S(2)}, u32[]{:S(2)}) async-start(bf16[32,2,6144]{2,1,0:T(2,128)(2,1)} %reshape.338), calls=%async_computation.2 | async-start | bytes 1572864 | tf_op jit(solution)/shard_map/all_to_all | solution.py:74
  119.8 16.2 %all-to-all-done.2 = bf16[32,2,6144]{2,1,0:T(2,128)(2,1)S(1)} async-done(((bf16[32,2,6144]{2,1,0:T(2,128)(2,1)}), bf16[32,2,6144]{2,1,0:T(2,128)(2,1)S(1)}, u32[]{:S(2)}, u32[]{:S(2)}) %all-to-all-start.2) | async-done | bytes 786464 | tf_op jit(solution)/shard_map/all_to_all | solution.py:74
  136.0 8.7 %all-to-all-start.4 = ((bf16[32,2,6144]{2,1,0:T(2,128)(2,1)}), bf16[32,2,6144]{2,1,0:T(2,128)(2,1)}, u32[]{:S(2)}, u32[]{:S(2)}) async-start(bf16[32,2,6144]{2,1,0:T(2,128)(2,1)} %reshape.342), calls=%async_computation.4 | async-start | bytes 1572864 | tf_op jit(solution)/shard_map/all_to_all | solution.py:73
  148.5 3.5 %convert_element_type.82 = bf16[192,2048]{1,0:T(8,128)(2,1)} reshape(bf16[32,6,32,64]{3,2,1,0:T(8,128)(2,1)} %copy.139) | data formatting | bytes 1572864 | tf_op jit(solution)/shard_map/convert_element_type | solution.py:94
  152.0 11.1 %all-to-all-done.4 = bf16[32,2,6144]{2,1,0:T(2,128)(2,1)} async-done(((bf16[32,2,6144]{2,1,0:T(2,128)(2,1)}), bf16[32,2,6144]{2,1,0:T(2,128)(2,1)}, u32[]{:S(2)}, u32[]{:S(2)}) %all-to-all-start.4) | async-done | bytes 786464 | tf_op jit(solution)/shard_map/all_to_all | solution.py:73
  163.1 3.8 %reshape.343 = bf16[32,6,32,64]{3,2,1,0:T(8,128)(2,1)} reshape(bf16[32,2,6144]{2,1,0:T(2,128)(2,1)} %all-to-all-done.4) | data formatting | bytes 1572864
  166.9 3.6 %copy.142 = bf16[32,6,32,64]{3,2,1,0:T(8,128)(2,1)} copy(bf16[32,6,32,64]{3,0,1,2:T(8,128)(2,1)} %bitcast.93) | data formatting | bytes 1572864 | tf_op jit(solution)/shard_map/all_to_all | solution.py:73
  170.5 2.8 reshape.251
  173.3 2.6 copy.146
  175.8 2.9 reshape.261
  183.6 8.8 %all-to-all-start.7 = ((f32[32,1,192]{2,1,0:T(1,128)}), f32[32,1,192]{2,1,0:T(1,128)}, u32[]{:S(2)}, u32[]{:S(2)}) async-start(f32[32,1,192]{2,1,0:T(1,128)} %reshape.348), calls=%async_computation.7 | async-start | bytes 65536 | tf_op jit(solution)/shard_map/all_to_all | solution.py:112
  197.6 5.4 %copy.163 = f32[32,6,32,64]{3,0,1,2:T(8,128)} copy(f32[32,6,32,64]{3,2,1,0:T(8,128)} %reshape.252) | data formatting | bytes 3145728 | tf_op jit(solution)/shard_map/reshape | solution.py:106
  203.0 4.4 %reshape.344 = f32[32,1,12288]{2,1,0:T(1,128)} reshape(f32[32,6,32,64]{3,2,1,0:T(8,128)} %bitcast.92) | data formatting | bytes 3145728
  207.4 8.9 %all-to-all-start.5 = ((f32[32,1,12288]{2,1,0:T(1,128)}), f32[32,1,12288]{2,1,0:T(1,128)S(1)}, u32[]{:S(2)}, u32[]{:S(2)}) async-start(f32[32,1,12288]{2,1,0:T(1,128)} %reshape.344), calls=%async_computation.5 | async-start | bytes 3145728 | tf_op jit(solution)/shard_map/all_to_all | solution.py:111
  219.2 34.4 %all-to-all-done.5 = f32[32,1,12288]{2,1,0:T(1,128)S(1)} async-done(((f32[32,1,12288]{2,1,0:T(1,128)}), f32[32,1,12288]{2,1,0:T(1,128)S(1)}, u32[]{:S(2)}, u32[]{:S(2)}) %all-to-all-start.5) | async-done | bytes 1572896 | tf_op jit(solution)/shard_map/all_to_all | solution.py:111
  253.6 7.4 %all-to-all-start.8 = ((f32[32,1,48]{2,1,0:T(1,128)}), f32[32,1,48]{2,1,0:T(1,128)S(1)}, u32[]{:S(2)}, u32[]{:S(2)}) async-start(f32[32,1,48]{2,1,0:T(1,128)} %copy.149), calls=%async_computation.8 | async-start | bytes 32768 | tf_op jit(solution)/shard_map/all_to_all | solution.py:122
  261.0 6.0 %reduce.8 = f32[32,12288]{1,0:T(8,128)} reduce(f32[32,1,12288]{2,1,0:T(1,128)S(1)} %all-to-all-done.5, f32[]{:T(128)} %broadcast.217), dimensions={1}, to_apply=%all_to_all.39.reduce_sub_computation | reduce | bytes 3145732 | tf_op jit(solution)/shard_map/all_to_all | solution.py:111
  267.0 3.6 %reshape.345 = f32[32,6,32,64]{3,2,1,0:T(8,128)} reshape(f32[32,12288]{1,0:T(8,128)} %reduce.8) | data formatting | bytes 3145728
  274.7 12.4 %all-to-all-start.6 = ((f32[32,1,3072]{2,1,0:T(1,128)}), f32[32,1,3072]{2,1,0:T(1,128)S(1)}, u32[]{:S(2)}, u32[]{:S(2)}) async-start(f32[32,1,3072]{2,1,0:T(1,128)} %reshape.346), calls=%async_computation.6 | async-start | bytes 786432 | tf_op jit(solution)/shard_map/all_to_all | solution.py:121
  289.7 4.5 %gather_fusion.4 = f32[768]{0:T(1024)S(1)} fusion(f32[1536]{0:T(1024)S(1)} %reshape.258, s32[1024]{0:T(1024)S(1)} %pad_clamp_fusion.2), kind=kCustom, calls=%fused_computation.4 | custom fusion | bytes 9216 | tf_op jit(solution)/shard_map/gather | solution.py:128
  294.9 20.2 %all-to-all-done.6 = f32[32,1,3072]{2,1,0:T(1,128)S(1)} async-done(((f32[32,1,3072]{2,1,0:T(1,128)}), f32[32,1,3072]{2,1,0:T(1,128)S(1)}, u32[]{:S(2)}, u32[]{:S(2)}) %all-to-all-start.6) | async-done | bytes 393248 | tf_op jit(solution)/shard_map/all_to_all | solution.py:121
  (90 shorter events, 40.1 us)
Async XLA Ops:
  0.6 180.4 %copy-start = (bf16[1,2048,192]{1,2,0:T(8,128)(2,1)S(1)}, bf16[1,2048,192]{1,2,0:T(8,128)(2,1)}, u32[]{:S(2)}) copy-start(bf16[1,2048,192]{1,2,0:T(8,128)(2,1)} %param.11) | copy-start | bytes 2359300
  3.6 6.5 %copy-start.4 = (s32[96,8]{0,1:T(8,128)S(1)}, s32[96,8]{0,1:T(8,128)}, u32[]{:S(2)}) copy-start(s32[96,8]{0,1:T(8,128)} %param.10) | copy-start | bytes 9220
  3.6 10.2 %copy-start.7 = (bf16[96,8]{0,1:T(8,128)(2,1)S(1)}, bf16[96,8]{0,1:T(8,128)(2,1)}, u32[]{:S(2)}) copy-start(bf16[96,8]{0,1:T(8,128)(2,1)} %param.9) | copy-start | bytes 4612
  14.1 30.7 %copy-start.5 = (bf16[96,64]{0,1:T(8,128)(2,1)S(1)}, bf16[96,64]{0,1:T(8,128)(2,1)}, u32[]{:S(2)}) copy-start(bf16[96,64]{0,1:T(8,128)(2,1)} %param.8) | copy-start | bytes 36868
  14.1 30.8 %copy-start.6 = (bf16[96,64]{0,1:T(8,128)(2,1)S(1)}, bf16[96,64]{0,1:T(8,128)(2,1)}, u32[]{:S(2)}) copy-start(bf16[96,64]{0,1:T(8,128)(2,1)} %param.7) | copy-start | bytes 36868
  24.3 32.1 %all-to-all-start = ((bf16[32,1,48]{2,1,0:T(2,128)(2,1)}), bf16[32,1,48]{2,1,0:T(2,128)(2,1)S(1)}, u32[]{:S(2)}, u32[]{:S(2)}) async-start(bf16[32,1,48]{2,1,0:T(2,128)(2,1)} %all_to_all.44), calls=%async_computation | async-start | bytes 32768 | tf_op jit(solution)/shard_map/all_to_all | solution.py:63
  56.4 27.1 %all-to-all-start.1 = ((bf16[32,2,1536]{2,1,0:T(2,128)(2,1)}), bf16[32,2,1536]{2,1,0:T(2,128)(2,1)S(1)}, u32[]{:S(2)}, u32[]{:S(2)}) async-start(bf16[32,2,1536]{2,1,0:T(2,128)(2,1)} %reshape.336), calls=%async_computation.1 | async-start | bytes 393216 | tf_op jit(solution)/shard_map/all_to_all | solution.py:62
  83.5 24.0 %all-to-all-start.3 = ((bf16[32,2,1536]{2,1,0:T(2,128)(2,1)}), bf16[32,2,1536]{2,1,0:T(2,128)(2,1)S(1)}, u32[]{:S(2)}, u32[]{:S(2)}) async-start(bf16[32,2,1536]{2,1,0:T(2,128)(2,1)} %reshape.340), calls=%async_computation.3 | async-start | bytes 393216 | tf_op jit(solution)/shard_map/all_to_all | solution.py:61
  107.5 28.5 %all-to-all-start.2 = ((bf16[32,2,6144]{2,1,0:T(2,128)(2,1)}), bf16[32,2,6144]{2,1,0:T(2,128)(2,1)S(1)}, u32[]{:S(2)}, u32[]{:S(2)}) async-start(bf16[32,2,6144]{2,1,0:T(2,128)(2,1)} %reshape.338), calls=%async_computation.2 | async-start | bytes 1572864 | tf_op jit(solution)/shard_map/all_to_all | solution.py:74
  136.0 27.1 %all-to-all-start.4 = ((bf16[32,2,6144]{2,1,0:T(2,128)(2,1)}), bf16[32,2,6144]{2,1,0:T(2,128)(2,1)}, u32[]{:S(2)}, u32[]{:S(2)}) async-start(bf16[32,2,6144]{2,1,0:T(2,128)(2,1)} %reshape.342), calls=%async_computation.4 | async-start | bytes 1572864 | tf_op jit(solution)/shard_map/all_to_all | solution.py:73
  178.8 1.8 copy-start.2
  181.0 1.1 copy-start.1
  183.6 23.8 %all-to-all-start.7 = ((f32[32,1,192]{2,1,0:T(1,128)}), f32[32,1,192]{2,1,0:T(1,128)}, u32[]{:S(2)}, u32[]{:S(2)}) async-start(f32[32,1,192]{2,1,0:T(1,128)} %reshape.348), calls=%async_computation.7 | async-start | bytes 65536 | tf_op jit(solution)/shard_map/all_to_all | solution.py:112
  207.4 46.2 %all-to-all-start.5 = ((f32[32,1,12288]{2,1,0:T(1,128)}), f32[32,1,12288]{2,1,0:T(1,128)S(1)}, u32[]{:S(2)}, u32[]{:S(2)}) async-start(f32[32,1,12288]{2,1,0:T(1,128)} %reshape.344), calls=%async_computation.5 | async-start | bytes 3145728 | tf_op jit(solution)/shard_map/all_to_all | solution.py:111
  253.6 21.1 %all-to-all-start.8 = ((f32[32,1,48]{2,1,0:T(1,128)}), f32[32,1,48]{2,1,0:T(1,128)S(1)}, u32[]{:S(2)}, u32[]{:S(2)}) async-start(f32[32,1,48]{2,1,0:T(1,128)} %copy.149), calls=%async_computation.8 | async-start | bytes 32768 | tf_op jit(solution)/shard_map/all_to_all | solution.py:122
  272.9 14.2 %copy-start.3 = (bf16[192,192]{1,0:T(8,128)(2,1)S(1)}, bf16[192,192]{1,0:T(8,128)(2,1)}, u32[]{:S(2)}) copy-start(bf16[192,192]{1,0:T(8,128)(2,1)} %get-tuple-element.38) | copy-start | bytes 221188
  274.7 40.4 %all-to-all-start.6 = ((f32[32,1,3072]{2,1,0:T(1,128)}), f32[32,1,3072]{2,1,0:T(1,128)S(1)}, u32[]{:S(2)}, u32[]{:S(2)}) async-start(f32[32,1,3072]{2,1,0:T(1,128)} %reshape.346), calls=%async_computation.6 | async-start | bytes 786432 | tf_op jit(solution)/shard_map/all_to_all | solution.py:121
where the time goes:
time: 321 us; the launch traced here: 319 us
  waiting for transfers between devices  119 us (37%)
  starting transfers between devices  89.9 us (28%)
  local copies, waits for them, and re-layouts  86.8 us (27%)
  other arithmetic  13.7 us (4%)
  matrix products  8.12 us (3%)
    all_to_all x1, waiting for transfers between devices, body(): lax.all_to_all(send_back, 'local', split_axis=2, concat_axis=2, tiled=True)  34.4 us
    unnamed x38, local copies, waits for them, and re-layouts  23.8 us
    all_to_all x1, starting transfers between devices, body(): lax.all_to_all(send_weight, 'node', split_axis=0, concat_axis=0, tiled=True)  20.4 us
    all_to_all x1, waiting for transfers between devices, body(): lax.all_to_all(summed_input, 'node', split_axis=0, concat_axis=0, tiled=T...  20.2 us
    all_to_all x1, waiting for transfers between devices, body(): lax.all_to_all(send_grad, 'node', split_axis=0, concat_axis=0, tiled=True)  17.7 us
    all_to_all x1, waiting for transfers between devices, body(): lax.all_to_all(send_input, 'node', split_axis=0, concat_axis=0, tiled=True)  16.2 us
    all_to_all x1, waiting for transfers between devices, body(): lax.all_to_all(fan_grad, 'local', split_axis=2, concat_axis=2, tiled=True)  16.2 us
    all_to_all x1, starting transfers between devices, body(): lax.all_to_all(summed_input, 'node', split_axis=0, concat_axis=0, tiled=T...  12.4 us
  transfers between devices with their start and end apart: 9, of which 7 were waited for; matrix products, arithmetic and copies ran while one was open for 19% of the time, Pallas kernels for 0%

commit v1 on v0

v1 whole, which is shorter than its diff:
```python
import functools

import jax
import jax.numpy as jnp
from jax import lax
from jax.experimental import pallas as pl
from jax.experimental.pallas import tpu as pltpu
from jax.sharding import PartitionSpec as P

MESH = pl.DeviceIdType.MESH
BF16, F32 = jnp.bfloat16, jnp.float32
NZ, LOCAL, CAP, GROUPS, TOP = 16, 32, 6, 8, 8
CHUNKS, PER = 4, 4
BLOCK = CAP * GROUPS
ROWS = 2 * NZ * CAP
LANES, TOK, FEAT = 128, 96, 64
WIDTH, QUARTER = LOCAL * FEAT, 192
EXTRA = 16
NT = (((1,), (1,)), ((), ()))
TN = (((0,), (0,)), ((), ()))


def along(k):
    odd = lax.rem(k, 2)
    half = lax.div(k + 1, 2)
    return (2 * odd - 1) * half


def dot(a, b, dims=(((1,), (0,)), ((), ()))):
    return lax.dot_general(a, b, dims, preferred_element_type=F32)


def relabel(slots, z, c):
    node = slots >> 3
    o = (z - (node >> 1)) & (NZ - 1)
    o = jnp.where(o > NZ // 2, o - NZ, o)
    k = jnp.where(o > 0, 2 * o - 1, -2 * o)
    return k, (node + c) & 1, slots & 7


def masks(rel, count):
    ids = lax.broadcasted_iota(jnp.int32, (count, LANES), 0)
    named = jnp.zeros((count, LANES), F32)
    for kk in range(TOP):
        named = named + jnp.where(rel[kk : kk + 1, :] == ids, 1.0, 0.0)
    row = lax.broadcasted_iota(jnp.int32, (LANES, LANES), 0)
    col = lax.broadcasted_iota(jnp.int32, (LANES, LANES), 1)
    earlier = jnp.where(row < col, 1.0, 0.0).astype(BF16)
    before = dot(named.astype(BF16), earlier)
    return [jnp.where(before == float(r), named, 0.0) for r in range(CAP)]


def stacked(parts, count):
    return jnp.stack([m.reshape(count // 8, 8, LANES) for m in parts], axis=1).reshape(
        count * CAP, LANES
    )


def kernel(
    tok, grd, prb, slt, wg_hbm, wu_hbm, wd_hbm,
    dtok, dprob, gg_hbm,
    wg, wu, wd, ggv, slot_own, slot_sib, tok_pad, grd_pad,
    send1, recv1, relay, send2, recv2, xs, gs, send3, recv3, zs, ptab,
    send4, recv4, sendx, recvx, home_own, home_sib,
    w_sem, gg_sem, sib_sem, s1, r1, s2, r2, s3, r3, s4, r4, x_sem,
):
    node, loc = lax.axis_index("node"), lax.axis_index("local")
    z, c = lax.div(node, 2), lax.rem(node, 2)
    sibling = 2 * z + lax.rem(c + 1, 2)

    def z_at(distance):
        return lax.rem(z + distance + NZ, NZ)

    weight_copies = [
        pltpu.make_async_copy(src.at[0], dst, w_sem.at[i])
        for i, (src, dst) in enumerate(((wg_hbm, wg), (wu_hbm, wu), (wd_hbm, wd)))
    ]
    for copy in weight_copies:
        copy.start()

    barrier = pltpu.get_barrier_semaphore()

    @pl.loop(1, 2 * NZ)
    def _(p):
        pl.semaphore_signal(
            barrier, inc=1, device_id=(lax.rem(node + p, 2 * NZ), loc), device_id_type=MESH
        )

    @pl.loop(1, LOCAL)
    def _(p):
        pl.semaphore_signal(
            barrier, inc=1, device_id=(node, lax.rem(loc + p, LOCAL)), device_id_type=MESH
        )

    slot_own[...] = jnp.full((TOP, LANES), -1, jnp.int32)
    slot_own[:, :TOK] = slt[...]
    own_slots = slot_own[...]
    k, j, g = relabel(own_slots, z, c)
    rel = jnp.where(own_slots < 0, -1, (k >> 2) * 64 + j * 32 + (k & 3) * 8 + g)
    rel0 = jnp.where((own_slots < 0) | (j > 0), -1, k * 8 + g)
    weights = jnp.concatenate(
        [prb[...].astype(F32), jnp.zeros((TOP, LANES - TOK), F32)], axis=1
    )
    count = 2 * NZ * GROUPS
    parts = masks(rel, count)
    ids = lax.broadcasted_iota(jnp.int32, (count, LANES), 0)
    scale = jnp.zeros((count, LANES), F32)
    for kk in range(TOP):
        scale = scale + jnp.where(rel[kk : kk + 1, :] == ids, weights[kk : kk + 1, :], 0.0)
    pick = stacked(parts, count)
    pick_scaled = stacked([m * scale for m in parts], count)
    tok_pad[...] = jnp.zeros((2 * FEAT, LANES), BF16)
    grd_pad[...] = jnp.zeros((2 * FEAT, LANES), BF16)
    tok_pad[:FEAT, :TOK] = tok[...]
    grd_pad[FEAT:, :TOK] = grd[...]
    rows = dot(pick.astype(BF16), tok_pad[...], NT) + dot(
        pick_scaled.astype(BF16), grd_pad[...], NT
    )
    send1[...] = rows.astype(BF16).reshape(2 * NZ, BLOCK, LANES)

    pl.semaphore_wait(barrier, 2 * NZ - 1 + LOCAL - 1)

    def block_of(k, j):
        return lax.div(k, PER) * (2 * PER) + j * PER + lax.rem(k, PER)

    sib_copy = pltpu.make_async_remote_copy(
        slot_own, slot_sib, sib_sem.at[0], sib_sem.at[1],
        device_id=(sibling, loc), device_id_type=MESH,
    )
    own1 = pltpu.make_async_copy(send1.at[0], recv1.at[0], r1.at[0])
    own1.start()

    @pl.loop(1, 2 * NZ)
    def _(t):
        k, j = lax.div(t, 2), lax.rem(t, 2)
        b = block_of(k, j)
        to = 2 * z_at(-along(k)) + lax.rem(c + j, 2)
        pltpu.make_async_remote_copy(
            send1.at[b], recv1.at[b], s1, r1.at[lax.div(k, PER)],
            device_id=(to, loc), device_id_type=MESH,
        ).start()

    sib_copy.start()

    for i in range(CHUNKS):
        chunk = recv1.at[pl.ds(8 * i, 8)]
        pltpu.make_async_copy(chunk, chunk, r1.at[i]).wait()
        relay[...] = chunk[...].reshape(8 * BLOCK, LANES).astype(F32)
        for g in range(GROUPS):
            send2[i, g] = relay[pl.ds(g, BLOCK, stride=8), :].astype(BF16)
        pltpu.make_async_copy(
            send2.at[i, lax.div(loc, 4)], recv2.at[i, loc], r2.at[i]
        ).start()

        @pl.loop(1, LOCAL)
        def _(p):
            to = lax.rem(loc + p, LOCAL)
            pltpu.make_async_remote_copy(
                send2.at[i, lax.div(to, 4)], recv2.at[i, loc], s2.at[i], r2.at[i],
                device_id=(node, to), device_id_type=MESH,
            ).start()

    home_own[...] = stacked(masks(rel0, NZ * GROUPS), NZ * GROUPS).astype(BF16)
    sib_copy.wait()
    sib_slots = slot_sib[...]
    k, j, g = relabel(sib_slots, z, c)
    rel1 = jnp.where((sib_slots < 0) | (j > 0), -1, k * 8 + g)
    home_sib[...] = stacked(masks(rel1, NZ * GROUPS), NZ * GROUPS).astype(BF16)
    send3[:, TOK:, :] = jnp.zeros((LOCAL, EXTRA, LANES), BF16)

    for copy in weight_copies:
        copy.wait()
    for i in range(CHUNKS):
        pltpu.make_async_copy(recv2.at[i], recv2.at[i], r2.at[i]).wait()
        here = slice(BLOCK * i, BLOCK * (i + 1))
        for p in range(LOCAL // 2):
            a, b = recv2[i, 2 * p], recv2[i, 2 * p + 1]
            there = slice(LANES * p, LANES * (p + 1))
            xs[here, there] = jnp.concatenate([a[:, :FEAT], b[:, :FEAT]], axis=1)
            gs[here, there] = jnp.concatenate([a[:, FEAT:], b[:, FEAT:]], axis=1)

    gate = dot(xs[...], wg[...], NT)
    up = dot(xs[...], wu[...], NT)
    d_hidden = dot(gs[...], wd[...], NT)
    sig = jax.nn.sigmoid(gate)
    silu = gate * sig
    hidden = (silu * up).astype(BF16).astype(F32)
    d_gate = (d_hidden * up * (sig * (1.0 + gate * (1.0 - sig)))).astype(BF16)
    d_up = (d_hidden * silu).astype(BF16)

    def halves(v):
        lower = [v[BLOCK * i : BLOCK * i + BLOCK // 2] for i in range(CHUNKS)]
        upper = [v[BLOCK * i + BLOCK // 2 : BLOCK * (i + 1)] for i in range(CHUNKS)]
        return jnp.concatenate(lower, axis=0), jnp.concatenate(upper, axis=0)

    ones = jnp.ones((8, QUARTER), F32)
    terms = []
    for half in halves(hidden * d_hidden):
        full = jnp.concatenate([half, jnp.zeros((LANES - TOK, QUARTER), F32)], axis=0)
        terms.append(
            lax.dot_general(
                ones, full, NT, precision=lax.Precision.HIGHEST, preferred_element_type=F32
            )[:1]
        )
    high = [t.astype(BF16) for t in terms]
    low = [(t - h.astype(F32)).astype(BF16) for t, h in zip(terms, high)]
    extra = jnp.concatenate(
        [v.astype(F32) for v in high + low] + [jnp.zeros((EXTRA - 4, LANES), F32)], axis=0
    ).astype(BF16)

    @pl.loop(0, LOCAL)
    def _(l):
        send3[l, TOK:, :] = extra

    for p in range(LOCAL // 4):
        there = slice(256 * p, 256 * (p + 1))
        part = dot(d_gate, wg[:, there]) + dot(d_up, wu[:, there])
        lower, upper = halves(part)
        lower, upper = lower.astype(BF16), upper.astype(BF16)
        for q in range(4):
            f = slice(FEAT * q, FEAT * (q + 1))
            send3[4 * p + q, :TOK, :] = jnp.concatenate([lower[:, f], upper[:, f]], axis=1)

    pltpu.make_async_copy(send3.at[loc], recv3.at[loc], r3.at[lax.div(loc, 4)]).start()

    @pl.loop(1, LOCAL)
    def _(p):
        to = lax.rem(loc + p, LOCAL)
        pltpu.make_async_remote_copy(
            send3.at[to], recv3.at[loc], s3, r3.at[lax.div(loc, 4)],
            device_id=(node, to), device_id_type=MESH,
        ).start()

    for p in range(LOCAL // 4):
        there = slice(256 * p, 256 * (p + 1))
        ggv[:, there] = dot(d_gate, xs[:, there], TN).astype(BF16)
    gg_copy = pltpu.make_async_copy(ggv, gg_hbm.at[0], gg_sem)
    gg_copy.start()

    for g in range(GROUPS):
        four = recv3.at[pl.ds(4 * g, 4)]
        pltpu.make_async_copy(four, four, r3.at[g]).wait()
        total = jnp.sum(four[...].astype(F32), axis=0)
        zs[pl.ds(g, TOK, stride=8), :] = total[:TOK]
        prob = total[TOK : TOK + 2] + total[TOK + 2 : TOK + 4]
        ptab[g : g + 1, :] = prob[:1]
        ptab[GROUPS + g : GROUPS + g + 1, :] = prob[1:]
    table = ptab[...].astype(BF16)
    send4[:, :BLOCK, :] = zs[...].reshape(NZ, BLOCK, LANES).astype(BF16)

    @pl.loop(0, NZ)
    def _(k):
        send4[k, BLOCK:, :] = table

    pltpu.make_async_copy(send4.at[0], recv4.at[0], r4).start()

    @pl.loop(1, NZ)
    def _(k):
        pltpu.make_async_remote_copy(
            send4.at[k], recv4.at[k], s4, r4,
            device_id=(2 * z_at(along(k)) + c, loc), device_id_type=MESH,
        ).start()

    pltpu.make_async_copy(recv4, recv4, r4).wait()
    back = recv4[:, :BLOCK, :].reshape(NZ * BLOCK, LANES)

    def prob_rows(home, names, first):
        sums = [jnp.zeros((8, LANES), F32) for _ in range(TOP)]
        groups = lax.broadcasted_iota(jnp.int32, (8, LANES), 0)
        for k in range(NZ):
            values = recv4[k, BLOCK:, :].astype(F32)[first : first + 8]
            hot = home[BLOCK * k : BLOCK * (k + 1), :].astype(F32).reshape(CAP, 8, LANES)
            found = jnp.zeros((8, LANES), F32)
            for r in range(CAP):
                found = found + hot[r] * values[:, CAP * k + r : CAP * k + r + 1]
            for kk in range(TOP):
                sums[kk] = sums[kk] + jnp.where(
                    names[kk : kk + 1, :] == groups + 8 * k, found, 0.0
                )
        return jnp.concatenate([jnp.sum(s, axis=0, keepdims=True) for s in sums], axis=0)

    sendx[:FEAT, :] = dot(back, home_sib[...], TN)[FEAT:]
    sendx[FEAT:, :] = prob_rows(home_sib, rel1, 8)
    x_copy = pltpu.make_async_remote_copy(
        sendx, recvx, x_sem.at[0], x_sem.at[1], device_id=(sibling, loc), device_id_type=MESH
    )
    x_copy.start()
    mine = dot(back, home_own[...], TN)[:FEAT]
    probs_mine = prob_rows(home_own, rel0, 0)
    x_copy.wait()
    dtok[...] = (mine + recvx[:FEAT, :])[:, :TOK].astype(BF16)
    dprob[...] = (probs_mine + recvx[FEAT:, :])[:, :TOK] / prb[...].astype(F32)

    sent = recv1.at[pl.ds(0, 2 * NZ - 1)]
    pltpu.make_async_copy(sent, sent, s1).wait()
    for i in range(CHUNKS):
        sent = recv2.at[i, pl.ds(0, LOCAL - 1)]
        pltpu.make_async_copy(sent, sent, s2.at[i]).wait()
    sent = recv3.at[pl.ds(0, LOCAL - 1)]
    pltpu.make_async_copy(sent, sent, s3).wait()
    sent = recv4.at[pl.ds(0, NZ - 1)]
    pltpu.make_async_copy(sent, sent, s4).wait()
    gg_copy.wait()


def body(tokens, grad_out, probs, slot_of, w_gate, w_up, w_down):
    vmem, hbm = pl.BlockSpec(memory_space=pltpu.VMEM), pl.BlockSpec(memory_space=pl.ANY)
    dma = pltpu.SemaphoreType.DMA
    d_tokens, d_probs, gate_grad = pl.pallas_call(
        kernel,
        out_shape=(
            jax.ShapeDtypeStruct((FEAT, TOK), BF16),
            jax.ShapeDtypeStruct((TOP, TOK), F32),
            jax.ShapeDtypeStruct((1, QUARTER, WIDTH), BF16),
        ),
        in_specs=[vmem] * 4 + [hbm] * 3,
        out_specs=(vmem, vmem, hbm),
        scratch_shapes=[
            pltpu.VMEM((QUARTER, WIDTH), BF16),
            pltpu.VMEM((QUARTER, WIDTH), BF16),
            pltpu.VMEM((QUARTER, WIDTH), BF16),
            pltpu.VMEM((QUARTER, WIDTH), BF16),
            pltpu.VMEM((TOP, LANES), jnp.int32),
            pltpu.VMEM((TOP, LANES), jnp.int32),
            pltpu.VMEM((2 * FEAT, LANES), BF16),
            pltpu.VMEM((2 * FEAT, LANES), BF16),
            pltpu.VMEM((2 * NZ, BLOCK, LANES), BF16),
            pltpu.VMEM((2 * NZ, BLOCK, LANES), BF16),
            pltpu.VMEM((8 * BLOCK, LANES), F32),
            pltpu.VMEM((CHUNKS, GROUPS, BLOCK, LANES), BF16),
            pltpu.VMEM((CHUNKS, LOCAL, BLOCK, LANES), BF16),
            pltpu.VMEM((ROWS, WIDTH), BF16),
            pltpu.VMEM((ROWS, WIDTH), BF16),
            pltpu.VMEM((LOCAL, TOK + EXTRA, LANES), BF16),
            pltpu.VMEM((LOCAL, TOK + EXTRA, LANES), BF16),
            pltpu.VMEM((NZ * BLOCK, LANES), F32),
            pltpu.VMEM((2 * GROUPS, LANES), F32),
            pltpu.VMEM((NZ, BLOCK + EXTRA, LANES), BF16),
            pltpu.VMEM((NZ, BLOCK + EXTRA, LANES), BF16),
            pltpu.VMEM((FEAT + TOP, LANES), F32),
            pltpu.VMEM((FEAT + TOP, LANES), F32),
            pltpu.VMEM((NZ * BLOCK, LANES), BF16),
            pltpu.VMEM((NZ * BLOCK, LANES), BF16),
            dma((3,)),
            dma,
            dma((2,)),
            dma,
            dma((CHUNKS,)),
            dma((CHUNKS,)),
            dma((CHUNKS,)),
            dma,
            dma((GROUPS,)),
            dma,
            dma,
            dma((2,)),
        ],
        compiler_params=pltpu.CompilerParams(
            collective_id=0, has_side_effects=True, vmem_limit_bytes=60 * 1024 * 1024
        ),
    )(
        tokens.T, grad_out.T, probs.T, slot_of.T,
        jnp.swapaxes(w_gate, 1, 2), jnp.swapaxes(w_up, 1, 2), w_down,
    )
    return d_tokens.T, d_probs.T, jnp.swapaxes(gate_grad, 1, 2)


def solution(mesh):
    in_specs = (
        P("node", "local"),
        P("node", "local"),
        P("node", None),
        P("node", None),
        P(("node", "local"), None, None),
        P(("node", "local"), None, None),
        P(("node", "local"), None, None),
    )
    out_specs = (P("node", "local"), P("node", None), P(("node", "local"), None, None))
    return jax.shard_map(body, mesh=mesh, in_specs=in_specs, out_specs=out_specs, check_vma=False)
```

time: 321 us -> 116 us (0.36)
  waiting for transfers between devices: 119 us -> 0 us
  Pallas kernels: 0 us -> 111 us
  starting transfers between devices: 89.9 us -> 0 us
  local copies, waits for them, and re-layouts: 86.8 us -> 4.01 us
  other arithmetic: 13.7 us -> 0 us
  matrix products: 8.12 us -> 0 us
    all_to_all x9 -> x0, waiting for transfers between devices: 119 us -> none  [the longest x1 34.4 us: body(): lax.all_to_all(send_back, 'local', split_axis=2, concat_axis=2, tiled=True)]
    pallas_call x0 -> x1, Pallas kernels: none -> 111 us  [body(): pl.pallas_call(kernel, out_shape=(jax.ShapeDtypeStruct((FEAT, TOK), BF16)...]
    all_to_all x9 -> x0, starting transfers between devices: 89.9 us -> none  [the longest x1 20.4 us: body(): lax.all_to_all(send_weight, 'node', split_axis=0, concat_axis=0, tiled=True)]
    gather x10 -> x0, local copies, waits for them, and re-layouts: 28.5 us -> none  [the longest x1 9.46 us: body(): probs.reshape(pair_count)[safe]]
    unnamed x38 -> x5, local copies, waits for them, and re-layouts: 23.8 us -> 4.01 us
    convert_element_type x4 -> x0, local copies, waits for them, and re-layouts: 11.2 us -> none  [the longest x2 5.73 us: body(): (weight_rows.astype(jnp.float32)[:, None] * grad_rows.astype(jnp.float32)...]
    reshape x7 -> x0, local copies, waits for them, and re-layouts: 10.9 us -> none  [the longest x2 7.8 us: body(): input_part.reshape(node_count, capacity, local_count, width_local)]
    all_to_all x4 -> x0, other arithmetic: 9.68 us -> none  [the longest x1 5.98 us: body(): lax.all_to_all(send_back, 'local', split_axis=2, concat_axis=2, tiled=True)]
  transfers between devices with their start and end apart: 9 -> 0, of which waited for: 7 -> 0; matrix products, arithmetic and copies ran while one was open for 19% -> 0% of each run, Pallas kernels for 0% -> 0%
where the time goes in v1:
time: 116 us; the launch traced here: 115 us
  Pallas kernels  111 us (96%)
  local copies, waits for them, and re-layouts  4.01 us (3%)
    pallas_call x1, Pallas kernels, body(): pl.pallas_call(kernel, out_shape=(jax.ShapeDtypeStruct((FEAT, TOK), BF16)...  111 us
    unnamed x5, local copies, waits for them, and re-layouts  4.01 us

profile of v1, /device:TPU:1, one launch (start us, length us, event | category | flops | bytes accessed | tf_op | source)
XLA Modules:
  0.0 115.2 jit_solution(1964378748111596296)
XLA Ops:
  0.6 110.5 %shard_map.94 = (bf16[64,96]{1,0:T(8,128)(2,1)}, f32[8,96]{1,0:T(8,128)}, bf16[1,192,2048]{2,1,0:T(8,128)(2,1)}) custom-call(bf16[64,96]{1,0:T(8,128)(2,1)} %bitcast.12, bf16[64,96]{1,0:T(8,128)(2,1)} %bitcast.13, bf16[8,96]{1,0:T(8,128)(2,1)} %bitcast.17, s32[8,96]{1,0:T(8,128)} %bitcast.15, bf16[1,192,2048]{2,1,0:T(8,128)(2,1)} %bitcast.10, ...), custom_call_target="tpu_custom_call" | custom-call | tf_op jit(solution)/shard_map/pallas_call | solution.py:309
  111.2 0.0 copy-start
  111.2 1.3 %copy.13 = bf16[96,64]{0,1:T(8,128)(2,1)} copy(bf16[96,64]{0,1:T(8,128)(2,1)} %bitcast.14) | data formatting | bytes 24576
  112.5 0.0 copy-done
  112.5 0.6 copy.14
  113.1 2.1 %copy.15 = bf16[1,2048,192]{1,2,0:T(8,128)(2,1)} copy(bf16[1,2048,192]{1,2,0:T(8,128)(2,1)} %bitcast.9) | data formatting | bytes 1572864
Async XLA Ops:
  111.2 1.3 %copy-start = (f32[8,96]{1,0:T(8,128)S(1)}, f32[8,96]{1,0:T(8,128)}, u32[]{:S(2)}) copy-start(f32[8,96]{1,0:T(8,128)} %get-tuple-element.7) | copy-start | bytes 9220

commit v2 on v1

--- a/solution.py
+++ b/solution.py
@@ -13,9 +13,9 @@
 CHUNKS, PER = 4, 4
 BLOCK = CAP * GROUPS
 ROWS = 2 * NZ * CAP
+NX, NY = 4, 8
 LANES, TOK, FEAT = 128, 96, 64
 WIDTH, QUARTER = LOCAL * FEAT, 192
-EXTRA = 16
 NT = (((1,), (1,)), ((), ()))
 TN = (((0,), (0,)), ((), ()))
 
@@ -60,13 +60,27 @@
     tok, grd, prb, slt, wg_hbm, wu_hbm, wd_hbm,
     dtok, dprob, gg_hbm,
     wg, wu, wd, ggv, slot_own, slot_sib, tok_pad, grd_pad,
-    send1, recv1, relay, send2, recv2, xs, gs, send3, recv3, zs, ptab,
-    send4, recv4, sendx, recvx, home_own, home_sib,
-    w_sem, gg_sem, sib_sem, s1, r1, s2, r2, s3, r3, s4, r4, x_sem,
+    send1, recv1, relay, send2, recv2, xs, gs, send3, recvw, sendf, recv3, zs,
+    send4, recv4, sendx, recvx, home_own, home_sib, pown, pz, psum, pall, ptab,
+    w_sem, gg_sem, sib_sem, s1, r1, s2f, s2d, s2w, r2f, r2d, r2w,
+    s3d, s3w, s3f, r3w, r3, s4, r4, x_sem, spz, rpz, spa, rpa,
 ):
     node, loc = lax.axis_index("node"), lax.axis_index("local")
     z, c = lax.div(node, 2), lax.rem(node, 2)
     sibling = 2 * z + lax.rem(c + 1, 2)
+    x, y = lax.div(loc, NY), lax.rem(loc, NY)
+    h, m = lax.div(y, 4), lax.rem(y, 4)
+    m_low, m_high = lax.rem(m, 2), lax.div(m, 2)
+    partner = loc + 1 - 2 * m_low
+    pos_f = 3 * (1 - m_low) + 2 * m_high
+    pos_w = 3 * m_low + 2 * m_high
+    pos_d = 6 * (1 - m_high)
+
+    def place(y_at):
+        return lax.rem(y_at + 14 - 4 * h, NY)
+
+    def x_at(distance):
+        return lax.rem(x + distance, NX)
 
     def z_at(distance):
         return lax.rem(z + distance + NZ, NZ)
@@ -92,12 +106,15 @@
             barrier, inc=1, device_id=(node, lax.rem(loc + p, LOCAL)), device_id_type=MESH
         )
 
+    def seen(g):
+        return (((g & 1) + h) & 1) * 4 + (g >> 1)
+
     slot_own[...] = jnp.full((TOP, LANES), -1, jnp.int32)
     slot_own[:, :TOK] = slt[...]
     own_slots = slot_own[...]
     k, j, g = relabel(own_slots, z, c)
     rel = jnp.where(own_slots < 0, -1, (k >> 2) * 64 + j * 32 + (k & 3) * 8 + g)
-    rel0 = jnp.where((own_slots < 0) | (j > 0), -1, k * 8 + g)
+    rel0 = jnp.where((own_slots < 0) | (j > 0), -1, k * 8 + seen(g))
     weights = jnp.concatenate(
         [prb[...].astype(F32), jnp.zeros((TOP, LANES - TOK), F32)], axis=1
     )
@@ -142,39 +159,74 @@
 
     sib_copy.start()
 
+    def pass_on(i):
+        @pl.loop(0, NX)
+        def _(d):
+            source = x_at(NX - d)
+            part = recv2.at[i, source, pl.ds(pos_f, 3)]
+            pltpu.make_async_copy(part, part, r2f.at[i, source]).wait()
+            pltpu.make_async_remote_copy(
+                part, part, s2w.at[i], r2w.at[i],
+                device_id=(node, partner), device_id_type=MESH,
+            ).start()
+
     for i in range(CHUNKS):
         chunk = recv1.at[pl.ds(8 * i, 8)]
         pltpu.make_async_copy(chunk, chunk, r1.at[i]).wait()
         relay[...] = chunk[...].reshape(8 * BLOCK, LANES).astype(F32)
         for g in range(GROUPS):
             send2[i, g] = relay[pl.ds(g, BLOCK, stride=8), :].astype(BF16)
+
+        def give(x_to, h_to, member, pos, send_sem, recv_sem):
+            pltpu.make_async_remote_copy(
+                send2.at[i, 2 * x_to + h_to], recv2.at[i, x, pos], send_sem, recv_sem,
+                device_id=(node, NY * x_to + 4 * h_to + member), device_id_type=MESH,
+            ).start()
+
+        pos_same, pos_other = lax.rem(m + 6, NY), lax.rem(m + 2, NY)
+
+        @pl.loop(0, NX)
+        def _(d):
+            to = x_at(d)
+            give(to, 1 - h, 3 * (1 - m_high), pos_other, s2f.at[i], r2f.at[i, x])
+            give(to, 1 - h, lax.rem(5 - m, 4), pos_other, s2f.at[i], r2f.at[i, x])
+            give(to, h, 2 - m_high, pos_same, s2f.at[i], r2f.at[i, x])
+
         pltpu.make_async_copy(
-            send2.at[i, lax.div(loc, 4)], recv2.at[i, loc], r2.at[i]
-        ).start()
-
-        @pl.loop(1, LOCAL)
-        def _(p):
-            to = lax.rem(loc + p, LOCAL)
-            pltpu.make_async_remote_copy(
-                send2.at[i, lax.div(to, 4)], recv2.at[i, loc], s2.at[i], r2.at[i],
-                device_id=(node, to), device_id_type=MESH,
-            ).start()
+            send2.at[i, 2 * x + h], recv2.at[i, x, pos_same], r2d.at[i]
+        ).start()
+
+        @pl.loop(0, NX)
+        def _(d):
+            give(x_at(d), h, 2 * m_high + 1 - m_low, pos_same, s2d.at[i], r2d.at[i])
+
+        @pl.loop(1, NX)
+        def _(d):
+            give(x_at(d), h, m, pos_same, s2d.at[i], r2d.at[i])
+
+        if i > 0:
+            pass_on(i - 1)
+    pass_on(CHUNKS - 1)
 
     home_own[...] = stacked(masks(rel0, NZ * GROUPS), NZ * GROUPS).astype(BF16)
     sib_copy.wait()
     sib_slots = slot_sib[...]
     k, j, g = relabel(sib_slots, z, c)
-    rel1 = jnp.where((sib_slots < 0) | (j > 0), -1, k * 8 + g)
+    rel1 = jnp.where((sib_slots < 0) | (j > 0), -1, k * 8 + seen(g))
     home_sib[...] = stacked(masks(rel1, NZ * GROUPS), NZ * GROUPS).astype(BF16)
-    send3[:, TOK:, :] = jnp.zeros((LOCAL, EXTRA, LANES), BF16)
 
     for copy in weight_copies:
         copy.wait()
     for i in range(CHUNKS):
-        pltpu.make_async_copy(recv2.at[i], recv2.at[i], r2.at[i]).wait()
+        part = recv2.at[i, :, pl.ds(pos_d, 2)]
+        pltpu.make_async_copy(part, part, r2d.at[i]).wait()
+        part = recv2.at[i, :, pl.ds(pos_w, 3)]
+        pltpu.make_async_copy(part, part, r2w.at[i]).wait()
         here = slice(BLOCK * i, BLOCK * (i + 1))
         for p in range(LOCAL // 2):
-            a, b = recv2[i, 2 * p], recv2[i, 2 * p + 1]
+            first = 2 * p % NY
+            a = recv2[i, 2 * p // NY, place(first)]
+            b = recv2[i, 2 * p // NY, place(first + 1)]
             there = slice(LANES * p, LANES * (p + 1))
             xs[here, there] = jnp.concatenate([a[:, :FEAT], b[:, :FEAT]], axis=1)
             gs[here, there] = jnp.concatenate([a[:, FEAT:], b[:, FEAT:]], axis=1)
@@ -202,15 +254,16 @@
                 ones, full, NT, precision=lax.Precision.HIGHEST, preferred_element_type=F32
             )[:1]
         )
-    high = [t.astype(BF16) for t in terms]
-    low = [(t - h.astype(F32)).astype(BF16) for t, h in zip(terms, high)]
-    extra = jnp.concatenate(
-        [v.astype(F32) for v in high + low] + [jnp.zeros((EXTRA - 4, LANES), F32)], axis=0
-    ).astype(BF16)
-
-    @pl.loop(0, LOCAL)
-    def _(l):
-        send3[l, TOK:, :] = extra
+    pown[0:1, :] = terms[0]
+    pown[1:2, :] = terms[1]
+    pltpu.make_async_copy(pown, pz.at[0], rpz).start()
+
+    @pl.loop(1, NZ)
+    def _(k):
+        pltpu.make_async_remote_copy(
+            pown, pz.at[k], spz, rpz,
+            device_id=(2 * z_at(along(k)) + c, loc), device_id_type=MESH,
+        ).start()
 
     for p in range(LOCAL // 4):
         there = slice(256 * p, 256 * (p + 1))
@@ -219,17 +272,55 @@
         lower, upper = lower.astype(BF16), upper.astype(BF16)
         for q in range(4):
             f = slice(FEAT * q, FEAT * (q + 1))
-            send3[4 * p + q, :TOK, :] = jnp.concatenate([lower[:, f], upper[:, f]], axis=1)
-
-    pltpu.make_async_copy(send3.at[loc], recv3.at[loc], r3.at[lax.div(loc, 4)]).start()
-
-    @pl.loop(1, LOCAL)
-    def _(p):
-        to = lax.rem(loc + p, LOCAL)
+            send3[p // 2, place(4 * (p % 2) + q)] = jnp.concatenate(
+                [lower[:, f], upper[:, f]], axis=1
+            )
+
+    @pl.loop(0, NX)
+    def _(d):
+        to = x_at(d)
         pltpu.make_async_remote_copy(
-            send3.at[to], recv3.at[loc], s3, r3.at[lax.div(loc, 4)],
-            device_id=(node, to), device_id_type=MESH,
-        ).start()
+            send3.at[to, pl.ds(pos_w, 3)], recvw.at[to], s3w, r3w.at[to],
+            device_id=(node, partner), device_id_type=MESH,
+        ).start()
+
+    def give_back(src, x_to, y_to, slot, sem, send_sem):
+        pltpu.make_async_remote_copy(
+            src, recv3.at[slot], send_sem, r3.at[sem],
+            device_id=(node, NY * x_to + y_to), device_id_type=MESH,
+        ).start()
+
+    pltpu.make_async_copy(
+        send3.at[x, pos_d + m_low], recv3.at[3 * x + m_low], r3.at[x]
+    ).start()
+
+    @pl.loop(0, NX)
+    def _(d):
+        to = x_at(d)
+        give_back(
+            send3.at[to, pos_d + 1 - m_low], to, 4 * h + 2 * m_high + 1 - m_low,
+            3 * x + m_low, x, s3d,
+        )
+
+    @pl.loop(1, NX)
+    def _(d):
+        to = x_at(d)
+        give_back(send3.at[to, pos_d + m_low], to, y, 3 * x + m_low, x, s3d)
+
+    @pl.loop(0, NX)
+    def _(d):
+        to = x_at(d)
+        pltpu.make_async_copy(recvw.at[to], recvw.at[to], r3w.at[to]).wait()
+        for f in range(3):
+            own = send3[to, pos_f + f].astype(F32)
+            sendf[to, f] = (own + recvw[to, f].astype(F32)).astype(BF16)
+        for f in range(3):
+            s_to = lax.rem(pos_f + f + 2, NY)
+            other = lax.div(s_to, 4)
+            slot = (1 - other) * (3 * x + 2) + other * (3 * NX + 2 * x + m_high)
+            give_back(
+                sendf.at[to, f], to, lax.rem(s_to + 4 * h, NY), slot, NX * other + x, s3f
+            )
 
     for p in range(LOCAL // 4):
         there = slice(256 * p, 256 * (p + 1))
@@ -237,20 +328,28 @@
     gg_copy = pltpu.make_async_copy(ggv, gg_hbm.at[0], gg_sem)
     gg_copy.start()
 
+    pltpu.make_async_copy(pz, pz, rpz).wait()
+    lane = lax.broadcasted_iota(jnp.int32, (2, LANES), 1)
+    found = jnp.zeros((2, LANES), F32)
+    for k in range(NZ):
+        found = jnp.where((lane >= CAP * k) & (lane < CAP * (k + 1)), pz[k], found)
+    psum[...] = found
+    pltpu.make_async_copy(psum, pall.at[loc], rpa).start()
+
+    @pl.loop(1, LOCAL)
+    def _(p):
+        pltpu.make_async_remote_copy(
+            psum, pall.at[loc], spa, rpa,
+            device_id=(node, lax.rem(loc + p, LOCAL)), device_id_type=MESH,
+        ).start()
+
     for g in range(GROUPS):
-        four = recv3.at[pl.ds(4 * g, 4)]
-        pltpu.make_async_copy(four, four, r3.at[g]).wait()
-        total = jnp.sum(four[...].astype(F32), axis=0)
-        zs[pl.ds(g, TOK, stride=8), :] = total[:TOK]
-        prob = total[TOK : TOK + 2] + total[TOK + 2 : TOK + 4]
-        ptab[g : g + 1, :] = prob[:1]
-        ptab[GROUPS + g : GROUPS + g + 1, :] = prob[1:]
-    table = ptab[...].astype(BF16)
-    send4[:, :BLOCK, :] = zs[...].reshape(NZ, BLOCK, LANES).astype(BF16)
-
-    @pl.loop(0, NZ)
-    def _(k):
-        send4[k, BLOCK:, :] = table
+        size = 3 if g < NX else 2
+        first = 3 * g if g < NX else 3 * NX + 2 * (g - NX)
+        part = recv3.at[pl.ds(first, size)]
+        pltpu.make_async_copy(part, part, r3.at[g]).wait()
+        zs[pl.ds(g, TOK, stride=8), :] = jnp.sum(part[...].astype(F32), axis=0)
+    send4[...] = zs[...].reshape(NZ, BLOCK, LANES).astype(BF16)
 
     pltpu.make_async_copy(send4.at[0], recv4.at[0], r4).start()
 
@@ -261,14 +360,19 @@
             device_id=(2 * z_at(along(k)) + c, loc), device_id_type=MESH,
         ).start()
 
-    pltpu.make_async_copy(recv4, recv4, r4).wait()
-    back = recv4[:, :BLOCK, :].reshape(NZ * BLOCK, LANES)
+    pltpu.make_async_copy(pall, pall, rpa).wait()
+    for g in range(GROUPS):
+        at = 4 * (2 * (g % NX) + lax.rem(h + g // NX, 2))
+        four = pall[at] + pall[at + 1] + pall[at + 2] + pall[at + 3]
+        ptab[g : g + 1, :] = four[:1]
+        ptab[GROUPS + g : GROUPS + g + 1, :] = four[1:]
+
 
     def prob_rows(home, names, first):
         sums = [jnp.zeros((8, LANES), F32) for _ in range(TOP)]
         groups = lax.broadcasted_iota(jnp.int32, (8, LANES), 0)
         for k in range(NZ):
-            values = recv4[k, BLOCK:, :].astype(F32)[first : first + 8]
+            values = ptab[first : first + 8, :]
             hot = home[BLOCK * k : BLOCK * (k + 1), :].astype(F32).reshape(CAP, 8, LANES)
             found = jnp.zeros((8, LANES), F32)
             for r in range(CAP):
@@ -279,14 +383,17 @@
                 )
         return jnp.concatenate([jnp.sum(s, axis=0, keepdims=True) for s in sums], axis=0)
 
+    sendx[FEAT:, :] = prob_rows(home_sib, rel1, 8)
+    probs_mine = prob_rows(home_own, rel0, 0)
+
+    pltpu.make_async_copy(recv4, recv4, r4).wait()
+    back = recv4[...].reshape(NZ * BLOCK, LANES)
     sendx[:FEAT, :] = dot(back, home_sib[...], TN)[FEAT:]
-    sendx[FEAT:, :] = prob_rows(home_sib, rel1, 8)
     x_copy = pltpu.make_async_remote_copy(
         sendx, recvx, x_sem.at[0], x_sem.at[1], device_id=(sibling, loc), device_id_type=MESH
     )
     x_copy.start()
     mine = dot(back, home_own[...], TN)[:FEAT]
-    probs_mine = prob_rows(home_own, rel0, 0)
     x_copy.wait()
     dtok[...] = (mine + recvx[:FEAT, :])[:, :TOK].astype(BF16)
     dprob[...] = (probs_mine + recvx[FEAT:, :])[:, :TOK] / prb[...].astype(F32)
@@ -294,10 +401,19 @@
     sent = recv1.at[pl.ds(0, 2 * NZ - 1)]
     pltpu.make_async_copy(sent, sent, s1).wait()
     for i in range(CHUNKS):
-        sent = recv2.at[i, pl.ds(0, LOCAL - 1)]
-        pltpu.make_async_copy(sent, sent, s2.at[i]).wait()
-    sent = recv3.at[pl.ds(0, LOCAL - 1)]
-    pltpu.make_async_copy(sent, sent, s3).wait()
+        sent = recv2.at[i, :, pl.ds(0, 3)]
+        pltpu.make_async_copy(sent, sent, s2f.at[i]).wait()
+        pltpu.make_async_copy(sent, sent, s2w.at[i]).wait()
+        sent = recv2.at[i, 0, pl.ds(0, 7)]
+        pltpu.make_async_copy(sent, sent, s2d.at[i]).wait()
+    sent = recv3.at[pl.ds(0, 7)]
+    pltpu.make_async_copy(sent, sent, s3d).wait()
+    pltpu.make_async_copy(recvw, recvw, s3w).wait()
+    pltpu.make_async_copy(sendf, sendf, s3f).wait()
+    sent = pz.at[pl.ds(0, NZ - 1)]
+    pltpu.make_async_copy(sent, sent, spz).wait()
+    sent = pall.at[pl.ds(0, LOCAL - 1)]
+    pltpu.make_async_copy(sent, sent, spa).wait()
     sent = recv4.at[pl.ds(0, NZ - 1)]
     pltpu.make_async_copy(sent, sent, s4).wait()
     gg_copy.wait()
@@ -328,19 +444,25 @@
             pltpu.VMEM((2 * NZ, BLOCK, LANES), BF16),
             pltpu.VMEM((8 * BLOCK, LANES), F32),
             pltpu.VMEM((CHUNKS, GROUPS, BLOCK, LANES), BF16),
-            pltpu.VMEM((CHUNKS, LOCAL, BLOCK, LANES), BF16),
+            pltpu.VMEM((CHUNKS, NX, NY, BLOCK, LANES), BF16),
             pltpu.VMEM((ROWS, WIDTH), BF16),
             pltpu.VMEM((ROWS, WIDTH), BF16),
-            pltpu.VMEM((LOCAL, TOK + EXTRA, LANES), BF16),
-            pltpu.VMEM((LOCAL, TOK + EXTRA, LANES), BF16),
+            pltpu.VMEM((NX, NY, TOK, LANES), BF16),
+            pltpu.VMEM((NX, 3, TOK, LANES), BF16),
+            pltpu.VMEM((NX, 3, TOK, LANES), BF16),
+            pltpu.VMEM((5 * NX, TOK, LANES), BF16),
             pltpu.VMEM((NZ * BLOCK, LANES), F32),
-            pltpu.VMEM((2 * GROUPS, LANES), F32),
-            pltpu.VMEM((NZ, BLOCK + EXTRA, LANES), BF16),
-            pltpu.VMEM((NZ, BLOCK + EXTRA, LANES), BF16),
+            pltpu.VMEM((NZ, BLOCK, LANES), BF16),
+            pltpu.VMEM((NZ, BLOCK, LANES), BF16),
             pltpu.VMEM((FEAT + TOP, LANES), F32),
             pltpu.VMEM((FEAT + TOP, LANES), F32),
             pltpu.VMEM((NZ * BLOCK, LANES), BF16),
             pltpu.VMEM((NZ * BLOCK, LANES), BF16),
+            pltpu.VMEM((2, LANES), F32),
+            pltpu.VMEM((NZ, 2, LANES), F32),
+            pltpu.VMEM((2, LANES), F32),
+            pltpu.VMEM((LOCAL, 2, LANES), F32),
+            pltpu.VMEM((2 * GROUPS, LANES), F32),
             dma((3,)),
             dma,
             dma((2,)),
@@ -348,11 +470,22 @@
             dma((CHUNKS,)),
             dma((CHUNKS,)),
             dma((CHUNKS,)),
-            dma,
+            dma((CHUNKS,)),
+            dma((CHUNKS, NX)),
+            dma((CHUNKS,)),
+            dma((CHUNKS,)),
+            dma,
+            dma,
+            dma,
+            dma((NX,)),
             dma((GROUPS,)),
             dma,
             dma,
             dma((2,)),
+            dma,
+            dma,
+            dma,
+            dma,
         ],
         compiler_params=pltpu.CompilerParams(
             collective_id=0, has_side_effects=True, vmem_limit_bytes=60 * 1024 * 1024

time: 116 us -> 100 us (0.86)
  Pallas kernels: 111 us -> 95.3 us
    pallas_call x1, Pallas kernels: 111 us -> 95.3 us  [body(): pl.pallas_call(kernel, out_shape=(jax.ShapeDtypeStruct((FEAT, TOK), BF16)...]
where the time goes in v2:
time: 100 us
  Pallas kernels  95.3 us (95%)
  local copies, waits for them, and re-layouts  4.01 us (4%)
    pallas_call x1, Pallas kernels, body(): pl.pallas_call(kernel, out_shape=(jax.ShapeDtypeStruct((FEAT, TOK), BF16)...  95.3 us
    unnamed x5, local copies, waits for them, and re-layouts  4.01 us

profile of v2, /device:TPU:1, one launch (start us, length us, event | category | flops | bytes accessed | tf_op | source)
XLA Modules:
  0.0 100.0 jit_solution(11071857866534226823)
XLA Ops:
  0.6 95.3 %shard_map.94 = (bf16[64,96]{1,0:T(8,128)(2,1)}, f32[8,96]{1,0:T(8,128)}, bf16[1,192,2048]{2,1,0:T(8,128)(2,1)}) custom-call(bf16[64,96]{1,0:T(8,128)(2,1)} %bitcast.12, bf16[64,96]{1,0:T(8,128)(2,1)} %bitcast.13, bf16[8,96]{1,0:T(8,128)(2,1)} %bitcast.17, s32[8,96]{1,0:T(8,128)} %bitcast.15, bf16[1,192,2048]{2,1,0:T(8,128)(2,1)} %bitcast.10, ...), custom_call_target="tpu_custom_call" | custom-call | tf_op jit(solution)/shard_map/pallas_call | solution.py:425
  96.0 0.0 copy-start
  96.0 1.3 %copy.13 = bf16[96,64]{0,1:T(8,128)(2,1)} copy(bf16[96,64]{0,1:T(8,128)(2,1)} %bitcast.14) | data formatting | bytes 24576
  97.3 0.0 copy-done
  97.3 0.6 copy.14
  97.9 2.1 %copy.15 = bf16[1,2048,192]{1,2,0:T(8,128)(2,1)} copy(bf16[1,2048,192]{1,2,0:T(8,128)(2,1)} %bitcast.9) | data formatting | bytes 1572864
Async XLA Ops:
  96.0 1.3 %copy-start = (f32[8,96]{1,0:T(8,128)S(1)}, f32[8,96]{1,0:T(8,128)}, u32[]{:S(2)}) copy-start(f32[8,96]{1,0:T(8,128)} %get-tuple-element.7) | copy-start | bytes 9220

commit v3 on v2

--- a/solution.py
+++ b/solution.py
@@ -14,6 +14,7 @@
 BLOCK = CAP * GROUPS
 ROWS = 2 * NZ * CAP
 NX, NY = 4, 8
+META = 16
 LANES, TOK, FEAT = 128, 96, 64
 WIDTH, QUARTER = LOCAL * FEAT, 192
 NT = (((1,), (1,)), ((), ()))
@@ -50,6 +51,10 @@
     return [jnp.where(before == float(r), named, 0.0) for r in range(CAP)]
 
 
+def slot_index(distance):
+    return 2 * distance - 1 if distance > 0 else -2 * distance
+
+
 def stacked(parts, count):
     return jnp.stack([m.reshape(count // 8, 8, LANES) for m in parts], axis=1).reshape(
         count * CAP, LANES
@@ -59,10 +64,9 @@
 def kernel(
     tok, grd, prb, slt, wg_hbm, wu_hbm, wd_hbm,
     dtok, dprob, gg_hbm,
-    wg, wu, wd, ggv, slot_own, slot_sib, tok_pad, grd_pad,
-    send1, recv1, relay, send2, recv2, xs, gs, send3, recvw, sendf, recv3, zs,
+    wg, wu, wd, ggv, slot_own, prob_own, raw, gath, relay, send2, recv2, xs, gs, send3, recvw, sendf, recv3, zs,
     send4, recv4, sendx, recvx, home_own, home_sib, pown, pz, psum, pall, ptab,
-    w_sem, gg_sem, sib_sem, s1, r1, s2f, s2d, s2w, r2f, r2d, r2w,
+    w_sem, gg_sem, sz, rz, ssib, rsib, s2f, s2d, s2w, r2f, r2d, r2w,
     s3d, s3w, s3f, r3w, r3, s4, r4, x_sem, spz, rpz, spa, rpa,
 ):
     node, loc = lax.axis_index("node"), lax.axis_index("local")
@@ -94,10 +98,12 @@
 
     barrier = pltpu.get_barrier_semaphore()
 
-    @pl.loop(1, 2 * NZ)
+    pl.semaphore_signal(barrier, inc=1, device_id=(sibling, loc), device_id_type=MESH)
+
+    @pl.loop(1, NZ)
     def _(p):
         pl.semaphore_signal(
-            barrier, inc=1, device_id=(lax.rem(node + p, 2 * NZ), loc), device_id_type=MESH
+            barrier, inc=1, device_id=(2 * z_at(p - NZ) + c, loc), device_id_type=MESH
         )
 
     @pl.loop(1, LOCAL)
@@ -111,53 +117,79 @@
 
     slot_own[...] = jnp.full((TOP, LANES), -1, jnp.int32)
     slot_own[:, :TOK] = slt[...]
-    own_slots = slot_own[...]
-    k, j, g = relabel(own_slots, z, c)
-    rel = jnp.where(own_slots < 0, -1, (k >> 2) * 64 + j * 32 + (k & 3) * 8 + g)
-    rel0 = jnp.where((own_slots < 0) | (j > 0), -1, k * 8 + seen(g))
-    weights = jnp.concatenate(
-        [prb[...].astype(F32), jnp.zeros((TOP, LANES - TOK), F32)], axis=1
+    prob_own[...] = jnp.zeros((TOP, LANES), F32)
+    prob_own[:, :TOK] = prb[...].astype(F32)
+    raw[...] = jnp.zeros((2 * FEAT, LANES), BF16)
+    raw[:FEAT, :TOK] = tok[...]
+    raw[FEAT:, :TOK] = grd[...]
+    row = lax.broadcasted_iota(jnp.int32, (LANES, LANES), 0)
+    col = lax.broadcasted_iota(jnp.int32, (LANES, LANES), 1)
+    same = jnp.where(row == col, 1.0, 0.0).astype(BF16)
+    earlier = jnp.where(row < col, 1.0, 0.0).astype(BF16)
+    gath[0, :TOK, :] = dot(same, raw[...], NT)[:TOK].astype(BF16)
+    gath[0, TOK:, :] = jnp.concatenate(
+        [slot_own[...].astype(F32), prob_own[...]], axis=0
+    ).astype(BF16)
+
+    pl.semaphore_wait(barrier, NZ + LOCAL - 1)
+
+    def block_of(k, j):
+        return k // PER * (2 * PER) + j * PER + k % PER
+
+    def hand_on(distance, hops):
+        src = gath.at[block_of(slot_index(distance), 0)]
+        k = slot_index(distance - hops)
+        pltpu.make_async_remote_copy(
+            src, gath.at[block_of(k, 0)], sz, rz.at[k],
+            device_id=(2 * z_at(hops) + c, loc), device_id_type=MESH,
+        ).start()
+
+    def hand_over(distance):
+        k = slot_index(distance)
+        pltpu.make_async_remote_copy(
+            gath.at[block_of(k, 0)], gath.at[block_of(k, 1)], ssib, rsib.at[k // PER],
+            device_id=(sibling, loc), device_id_type=MESH,
+        ).start()
+
+    def arrived(distance):
+        k = slot_index(distance)
+        block = gath.at[block_of(k, 0)]
+        pltpu.make_async_copy(block, block, rz.at[k]).wait()
+
+    hand_over(0)
+    for hops in (3, -3, 1, -1, 6, -6):
+        hand_on(0, hops)
+
+    steps = (
+        ((1, ()), (-1, ()), (3, (1, -1)), (-3, (-1, 1)), (2, ())),
+        ((6, (1, -1, -2)), (-6, (-1, 1)), (-2, ()), (4, ())),
+        ((-4, ()), (5, ()), (-5, ())),
+        ((7, ()), (-7, ()), (8, ())),
     )
-    count = 2 * NZ * GROUPS
-    parts = masks(rel, count)
-    ids = lax.broadcasted_iota(jnp.int32, (count, LANES), 0)
-    scale = jnp.zeros((count, LANES), F32)
-    for kk in range(TOP):
-        scale = scale + jnp.where(rel[kk : kk + 1, :] == ids, weights[kk : kk + 1, :], 0.0)
-    pick = stacked(parts, count)
-    pick_scaled = stacked([m * scale for m in parts], count)
-    tok_pad[...] = jnp.zeros((2 * FEAT, LANES), BF16)
-    grd_pad[...] = jnp.zeros((2 * FEAT, LANES), BF16)
-    tok_pad[:FEAT, :TOK] = tok[...]
-    grd_pad[FEAT:, :TOK] = grd[...]
-    rows = dot(pick.astype(BF16), tok_pad[...], NT) + dot(
-        pick_scaled.astype(BF16), grd_pad[...], NT
-    )
-    send1[...] = rows.astype(BF16).reshape(2 * NZ, BLOCK, LANES)
-
-    pl.semaphore_wait(barrier, 2 * NZ - 1 + LOCAL - 1)
-
-    def block_of(k, j):
-        return lax.div(k, PER) * (2 * PER) + j * PER + lax.rem(k, PER)
-
-    sib_copy = pltpu.make_async_remote_copy(
-        slot_own, slot_sib, sib_sem.at[0], sib_sem.at[1],
-        device_id=(sibling, loc), device_id_type=MESH,
-    )
-    own1 = pltpu.make_async_copy(send1.at[0], recv1.at[0], r1.at[0])
-    own1.start()
-
-    @pl.loop(1, 2 * NZ)
-    def _(t):
-        k, j = lax.div(t, 2), lax.rem(t, 2)
-        b = block_of(k, j)
-        to = 2 * z_at(-along(k)) + lax.rem(c + j, 2)
-        pltpu.make_async_remote_copy(
-            send1.at[b], recv1.at[b], s1, r1.at[lax.div(k, PER)],
-            device_id=(to, loc), device_id_type=MESH,
-        ).start()
-
-    sib_copy.start()
+
+    def pick_rows(i):
+        want = (lax.broadcasted_iota(jnp.int32, (8, LANES), 0) + 8 * node).astype(F32)
+        lane = lax.broadcasted_iota(jnp.int32, (BLOCK, LANES), 1)
+        named, scaled = [], []
+        for b in range(8):
+            meta = gath[8 * i + b, TOK:, :].astype(F32)
+            hits, scale = jnp.zeros((8, LANES), F32), jnp.zeros((8, LANES), F32)
+            for kk in range(TOP):
+                hit = meta[kk : kk + 1, :] == want
+                hits = hits + jnp.where(hit, 1.0, 0.0)
+                scale = scale + jnp.where(hit, meta[TOP + kk : TOP + kk + 1, :], 0.0)
+            named.append(hits)
+            scaled.append(scale)
+        before = dot(jnp.concatenate(named, axis=0).astype(BF16), earlier)
+        for b in range(8):
+            rank = before[8 * b : 8 * b + 8]
+            plain = [jnp.where(rank == float(r), named[b], 0.0) for r in range(CAP)]
+            times = [jnp.where(rank == float(r), scaled[b], 0.0) for r in range(CAP)]
+            pick = jnp.concatenate(plain + times, axis=0).astype(BF16)
+            both = dot(pick[:, :TOK], gath[8 * i + b, :TOK, :])
+            relay[BLOCK * b : BLOCK * (b + 1), :] = jnp.where(
+                lane < FEAT, both[:BLOCK], both[BLOCK:]
+            )
 
     def pass_on(i):
         @pl.loop(0, NX)
@@ -171,9 +203,14 @@
             ).start()
 
     for i in range(CHUNKS):
-        chunk = recv1.at[pl.ds(8 * i, 8)]
-        pltpu.make_async_copy(chunk, chunk, r1.at[i]).wait()
-        relay[...] = chunk[...].reshape(8 * BLOCK, LANES).astype(F32)
+        for distance, onward in steps[i]:
+            arrived(distance)
+            for hops in onward:
+                hand_on(distance, hops)
+            hand_over(distance)
+        four = gath.at[pl.ds(8 * i + PER, PER)]
+        pltpu.make_async_copy(four, four, rsib.at[i]).wait()
+        pick_rows(i)
         for g in range(GROUPS):
             send2[i, g] = relay[pl.ds(g, BLOCK, stride=8), :].astype(BF16)
 
@@ -208,9 +245,11 @@
             pass_on(i - 1)
     pass_on(CHUNKS - 1)
 
+    own_slots = slot_own[...]
+    k, j, g = relabel(own_slots, z, c)
+    rel0 = jnp.where((own_slots < 0) | (j > 0), -1, k * 8 + seen(g))
     home_own[...] = stacked(masks(rel0, NZ * GROUPS), NZ * GROUPS).astype(BF16)
-    sib_copy.wait()
-    sib_slots = slot_sib[...]
+    sib_slots = gath[PER, TOK : TOK + TOP, :].astype(F32).astype(jnp.int32)
     k, j, g = relabel(sib_slots, z, c)
     rel1 = jnp.where((sib_slots < 0) | (j > 0), -1, k * 8 + seen(g))
     home_sib[...] = stacked(masks(rel1, NZ * GROUPS), NZ * GROUPS).astype(BF16)
@@ -398,8 +437,10 @@
     dtok[...] = (mine + recvx[:FEAT, :])[:, :TOK].astype(BF16)
     dprob[...] = (probs_mine + recvx[FEAT:, :])[:, :TOK] / prb[...].astype(F32)
 
-    sent = recv1.at[pl.ds(0, 2 * NZ - 1)]
-    pltpu.make_async_copy(sent, sent, s1).wait()
+    sent = gath.at[pl.ds(0, NZ - 1)]
+    pltpu.make_async_copy(sent, sent, sz).wait()
+    sent = gath.at[pl.ds(0, NZ)]
+    pltpu.make_async_copy(sent, sent, ssib).wait()
     for i in range(CHUNKS):
         sent = recv2.at[i, :, pl.ds(0, 3)]
         pltpu.make_async_copy(sent, sent, s2f.at[i]).wait()
@@ -437,11 +478,9 @@
             pltpu.VMEM((QUARTER, WIDTH), BF16),
             pltpu.VMEM((QUARTER, WIDTH), BF16),
             pltpu.VMEM((TOP, LANES), jnp.int32),
-            pltpu.VMEM((TOP, LANES), jnp.int32),
+            pltpu.VMEM((TOP, LANES), F32),
             pltpu.VMEM((2 * FEAT, LANES), BF16),
-            pltpu.VMEM((2 * FEAT, LANES), BF16),
-            pltpu.VMEM((2 * NZ, BLOCK, LANES), BF16),
-            pltpu.VMEM((2 * NZ, BLOCK, LANES), BF16),
+            pltpu.VMEM((2 * NZ, TOK + META, LANES), BF16),
             pltpu.VMEM((8 * BLOCK, LANES), F32),
             pltpu.VMEM((CHUNKS, GROUPS, BLOCK, LANES), BF16),
             pltpu.VMEM((CHUNKS, NX, NY, BLOCK, LANES), BF16),
@@ -465,7 +504,8 @@
             pltpu.VMEM((2 * GROUPS, LANES), F32),
             dma((3,)),
             dma,
-            dma((2,)),
+            dma,
+            dma((NZ,)),
             dma,
             dma((CHUNKS,)),
             dma((CHUNKS,)),

time: 100 us -> 103 us (1.030)
  Pallas kernels: 95.3 us -> 98.5 us
    pallas_call x1, Pallas kernels: 95.3 us -> 98.5 us  [body(): pl.pallas_call(kernel, out_shape=(jax.ShapeDtypeStruct((FEAT, TOK), BF16)...]
where the time goes in v3:
time: 103 us
  Pallas kernels  98.5 us (96%)
  local copies, waits for them, and re-layouts  4.01 us (4%)
    pallas_call x1, Pallas kernels, body(): pl.pallas_call(kernel, out_shape=(jax.ShapeDtypeStruct((FEAT, TOK), BF16)...  98.5 us
    unnamed x5, local copies, waits for them, and re-layouts  4.01 us

profile of v3, /device:TPU:1, one launch (start us, length us, event | category | flops | bytes accessed | tf_op | source)
XLA Modules:
  0.0 103.1 jit_solution(2539390806563751972)
XLA Ops:
  0.6 98.5 %shard_map.94 = (bf16[64,96]{1,0:T(8,128)(2,1)}, f32[8,96]{1,0:T(8,128)}, bf16[1,192,2048]{2,1,0:T(8,128)(2,1)}) custom-call(bf16[64,96]{1,0:T(8,128)(2,1)} %bitcast.12, bf16[64,96]{1,0:T(8,128)(2,1)} %bitcast.13, bf16[8,96]{1,0:T(8,128)(2,1)} %bitcast.17, s32[8,96]{1,0:T(8,128)} %bitcast.15, bf16[1,192,2048]{2,1,0:T(8,128)(2,1)} %bitcast.10, ...), custom_call_target="tpu_custom_call" | custom-call | tf_op jit(solution)/shard_map/pallas_call | solution.py:466
  99.1 0.0 copy-start
  99.1 1.3 %copy.13 = bf16[96,64]{0,1:T(8,128)(2,1)} copy(bf16[96,64]{0,1:T(8,128)(2,1)} %bitcast.14) | data formatting | bytes 24576
  100.5 0.0 copy-done
  100.5 0.6 copy.14
  101.1 2.1 %copy.15 = bf16[1,2048,192]{1,2,0:T(8,128)(2,1)} copy(bf16[1,2048,192]{1,2,0:T(8,128)(2,1)} %bitcast.9) | data formatting | bytes 1572864
Async XLA Ops:
  99.1 1.3 %copy-start = (f32[8,96]{1,0:T(8,128)S(1)}, f32[8,96]{1,0:T(8,128)}, u32[]{:S(2)}) copy-start(f32[8,96]{1,0:T(8,128)} %get-tuple-element.7) | copy-start | bytes 9220

commit v4 on v2

--- a/solution.py
+++ b/solution.py
@@ -58,7 +58,7 @@
 
 def kernel(
     tok, grd, prb, slt, wg_hbm, wu_hbm, wd_hbm,
-    dtok, dprob, gg_hbm,
+    small, gg_hbm,
     wg, wu, wd, ggv, slot_own, slot_sib, tok_pad, grd_pad,
     send1, recv1, relay, send2, recv2, xs, gs, send3, recvw, sendf, recv3, zs,
     send4, recv4, sendx, recvx, home_own, home_sib, pown, pz, psum, pall, ptab,
@@ -395,8 +395,8 @@
     x_copy.start()
     mine = dot(back, home_own[...], TN)[:FEAT]
     x_copy.wait()
-    dtok[...] = (mine + recvx[:FEAT, :])[:, :TOK].astype(BF16)
-    dprob[...] = (probs_mine + recvx[FEAT:, :])[:, :TOK] / prb[...].astype(F32)
+    small[:FEAT, :] = (mine + recvx[:FEAT, :])[:, :TOK]
+    small[FEAT:, :] = (probs_mine + recvx[FEAT:, :])[:, :TOK] / prb[...].astype(F32)
 
     sent = recv1.at[pl.ds(0, 2 * NZ - 1)]
     pltpu.make_async_copy(sent, sent, s1).wait()
@@ -422,15 +422,14 @@
 def body(tokens, grad_out, probs, slot_of, w_gate, w_up, w_down):
     vmem, hbm = pl.BlockSpec(memory_space=pltpu.VMEM), pl.BlockSpec(memory_space=pl.ANY)
     dma = pltpu.SemaphoreType.DMA
-    d_tokens, d_probs, gate_grad = pl.pallas_call(
+    small, gate_grad = pl.pallas_call(
         kernel,
         out_shape=(
-            jax.ShapeDtypeStruct((FEAT, TOK), BF16),
-            jax.ShapeDtypeStruct((TOP, TOK), F32),
+            jax.ShapeDtypeStruct((FEAT + TOP, TOK), F32),
             jax.ShapeDtypeStruct((1, QUARTER, WIDTH), BF16),
         ),
         in_specs=[vmem] * 4 + [hbm] * 3,
-        out_specs=(vmem, vmem, hbm),
+        out_specs=(vmem, hbm),
         scratch_shapes=[
             pltpu.VMEM((QUARTER, WIDTH), BF16),
             pltpu.VMEM((QUARTER, WIDTH), BF16),
@@ -494,7 +493,7 @@
         tokens.T, grad_out.T, probs.T, slot_of.T,
         jnp.swapaxes(w_gate, 1, 2), jnp.swapaxes(w_up, 1, 2), w_down,
     )
-    return d_tokens.T, d_probs.T, jnp.swapaxes(gate_grad, 1, 2)
+    return small[:FEAT].astype(BF16).T, small[FEAT:].T, jnp.swapaxes(gate_grad, 1, 2)
 
 
 def solution(mesh):

time: 100 us -> 101 us (1.010)
    transpose x0 -> x2, local copies, waits for them, and re-layouts: none -> 2.63 us  [the longest x1 1.37 us: body(): small[:FEAT].astype(BF16)]
    unnamed x5 -> x1, local copies, waits for them, and re-layouts: 4.01 us -> 2.09 us
where the time goes in v4:
time: 101 us
  Pallas kernels  95.2 us (94%)
  local copies, waits for them, and re-layouts  4.72 us (5%)
    pallas_call x1, Pallas kernels, body(): pl.pallas_call(kernel, out_shape=(jax.ShapeDtypeStruct((FEAT + TOP, TOK),...  95.2 us
    unnamed x1, local copies, waits for them, and re-layouts  2.09 us

profile of v4, /device:TPU:1, one launch (start us, length us, event | category | flops | bytes accessed | tf_op | source)
XLA Modules:
  0.0 100.6 jit_solution(6044023502916768467)
XLA Ops:
  0.6 95.2 %shard_map.94 = (f32[72,96]{1,0:T(8,128)}, bf16[1,192,2048]{2,1,0:T(8,128)(2,1)}) custom-call(bf16[64,96]{1,0:T(8,128)(2,1)} %bitcast.14, bf16[64,96]{1,0:T(8,128)(2,1)} %bitcast.15, bf16[8,96]{1,0:T(8,128)(2,1)} %bitcast.17, s32[8,96]{1,0:T(8,128)} %bitcast.16, bf16[1,192,2048]{2,1,0:T(8,128)(2,1)} %bitcast.12, bf16[1,192,2048]{2,1,0:T(8,128)(2,1)} %bitcast.13, ...), custom_call_target="tpu_custom_call" | custom-call | tf_op jit(solution)/shard_map/pallas_call | solution.py:425
  95.9 1.4 %fusion = bf16[96,64]{0,1:T(8,128)(2,1)} fusion(f32[72,96]{1,0:T(8,128)} %get-tuple-element.5), kind=kLoop, calls=%fused_computation.1 | loop fusion | bytes 24576 | tf_op jit(solution)/shard_map/transpose | solution.py:496
  97.2 1.3 %slice_bitcast_fusion = f32[96,8]{0,1:T(8,128)} fusion(f32[72,96]{1,0:T(8,128)} %get-tuple-element.5), kind=kLoop, calls=%fused_computation.2 | loop fusion | bytes 6144 | tf_op jit(solution)/shard_map/transpose | solution.py:496
  98.5 2.1 %copy.11 = bf16[1,2048,192]{1,2,0:T(8,128)(2,1)} copy(bf16[1,2048,192]{1,2,0:T(8,128)(2,1)} %bitcast.11) | data formatting | bytes 1572864
